TPU v7x, 32 devices: a whole 2x2x4 slice. The times are simulated.
32 devices in a mesh: groups: 2 (over x), rows: 16 (over z, y, core).
Axes of the slice: x: 2, y: 2, z: 4, core: 2. Of those that a mesh axis runs over, the one named last changes fastest.
Arguments:
- features: bfloat16 [128, 4, 3072], P(('groups', 'rows')), parts along dimension 0, may hold values from -6 to 6
- cotangent: bfloat16 [128, 4, 3072], P(('groups', 'rows')), parts along dimension 0, may hold values from -6 to 6
- depth_kernel: float32 [7, 7, 3072], replicated, may hold values from -0.875 to 0.875
- depth_bias: float32 [3072], replicated, may hold values from -3 to 3
- norm_gain: float32 [3072], replicated, may hold values from 0.1 to 1.9
- norm_shift: float32 [3072], replicated, may hold values from -3 to 3
- up_weight: bfloat16 [3072, 12288], P(None, 'rows'), may hold values from -0.109375 to 0.109375
- up_bias: float32 [12288], P('rows'), may hold values from -3 to 3
- down_weight: bfloat16 [12288, 3072], P('rows'), may hold values from -0.109375 to 0.109375
- layer_scale: float32 [3072], replicated, may hold values from 0.3 to 3
Outputs:
- input_grad: bfloat16 [128, 4, 3072], P(('groups', 'rows')), parts along dimension 0
- up_grad: float32 [6144, 12288], P('groups', 'rows'), parts along dimension 0
- up_bias_grad: float32 [24576], P(('groups', 'rows')), parts along dimension 0
- down_grad: float32 [24576, 3072], P(('groups', 'rows')), parts along dimension 0
- kernel_grad: float32 [14, 7, 3072], P('groups'), parts along dimension 0
- depth_bias_grad: float32 [6144], P('groups'), parts along dimension 0
- gain_grad: float32 [6144], P('groups'), parts along dimension 0
- shift_grad: float32 [6144], P('groups'), parts along dimension 0
There are 2 independent parts, one for each index of `groups`. A program takes and returns all parts, laid end to end along the dimension named above; an argument that names none is the same for every part. Nothing has to cross between parts.
All inputs are finite; a program needn't handle non-finite values.
Results may differ from a plain program's by a relative error of at most 0.0075.
Values may be sent and summed in bfloat16 or wider, within the bound.
No kernel may reach another device: no remote copies, remote signals or barrier semaphores. Data moves between devices by JAX's collectives and lax.ppermute only.
A program may use at most 128 MiB of HBM per device.

v0:
```python
import jax
import jax.numpy as jnp
from jax import lax
from jax.sharding import PartitionSpec as P

IMG_ROWS = 32


def extended(cells, sides, width):
    for axis, dim in sides:
        count = lax.axis_size(axis)
        head = lax.slice_in_dim(cells, 0, width, axis=dim)
        tail = lax.slice_in_dim(cells, cells.shape[dim] - width, cells.shape[dim], axis=dim)
        cells = jnp.concatenate(
            [
                lax.ppermute(tail, axis, [(i, (i + 1) % count) for i in range(count)]),
                cells,
                lax.ppermute(head, axis, [((i + 1) % count, i) for i in range(count)]),
            ],
            axis=dim,
        )
    return cells


def gelu_value(pre_act):
    return 0.5 * pre_act * (1.0 + jax.scipy.special.erf(pre_act * 0.7071067811865476))


def gelu_slope(pre_act):
    cdf_part = 0.5 * (1.0 + jax.scipy.special.erf(pre_act * 0.7071067811865476))
    return cdf_part + pre_act * jnp.exp(-0.5 * pre_act * pre_act) * 0.3989422804014327


def contract(left, right, left_dim, right_dim):
    return lax.dot_general(
        left, right, (((left_dim,), (right_dim,)), ((), ())), preferred_element_type=jnp.float32
    )


def depthwise(padded, kernel, offset_term, row_count, col_count):
    summed = jnp.zeros(padded[..., 3 : 3 + row_count, 3 : 3 + col_count, :].shape, padded.dtype)
    for tap_row in range(7):
        for tap_col in range(7):
            summed = (
                summed
                + kernel[tap_row, tap_col]
                * padded[..., tap_row : tap_row + row_count, tap_col : tap_col + col_count, :]
            )
    return summed + offset_term


def depthwise_back(padded_grad, kernel, row_count, col_count):
    summed = jnp.zeros(
        padded_grad[..., 3 : 3 + row_count, 3 : 3 + col_count, :].shape, padded_grad.dtype
    )
    for tap_row in range(7):
        for tap_col in range(7):
            summed = (
                summed
                + kernel[tap_row, tap_col]
                * padded_grad[
                    ...,
                    6 - tap_row : 6 - tap_row + row_count,
                    6 - tap_col : 6 - tap_col + col_count,
                    :,
                ]
            )
    return summed


def normalize(conv_out):
    row_mean = jnp.mean(conv_out, axis=-1, keepdims=True)
    centred = conv_out - row_mean
    inv_std = lax.rsqrt(jnp.mean(centred * centred, axis=-1, keepdims=True) + 1e-06)
    return (centred * inv_std, inv_std)


def norm_back(norm_grad, unit_norm, inv_std, norm_gain):
    scaled = norm_grad * norm_gain
    return inv_std * (
        scaled
        - jnp.mean(scaled, axis=-1, keepdims=True)
        - unit_norm * jnp.mean(scaled * unit_norm, axis=-1, keepdims=True)
    )


def pad_columns(block):
    return jnp.pad(block, ((0, 0), (3, 3), (0, 0)))


def on_device(
    features,
    cotangent,
    depth_kernel,
    depth_bias,
    norm_gain,
    norm_shift,
    up_weight,
    up_bias,
    down_weight,
    layer_scale,
):
    rows_dev, col_count, channels = features.shape
    total_rows = rows_dev * lax.axis_size("rows")
    half_image = IMG_ROWS // 2
    my_index = lax.axis_index("rows")
    first_row = my_index * rows_dev
    row_offsets = first_row - 3 + jnp.arange(rows_dev + 6, dtype=jnp.int32)
    row_image = jnp.mod(row_offsets - half_image, total_rows) // IMG_ROWS
    own_image = jnp.mod(first_row - half_image, total_rows) // IMG_ROWS
    row_mask = (row_image == own_image).astype(jnp.float32)[:, None, None]
    cot_scaled = (
        (cotangent.astype(jnp.float32) * layer_scale)
        .astype(jnp.bfloat16)
        .reshape(rows_dev * col_count, channels)
    )
    cot_all = lax.all_gather(cot_scaled, "rows", axis=0, tiled=True)
    near_rows = extended(features, (("rows", 0),), 3)
    padded = pad_columns(near_rows.astype(jnp.float32) * row_mask)
    conv_out = depthwise(padded, depth_kernel, depth_bias, rows_dev, col_count)
    unit_norm, inv_std = normalize(conv_out)
    normed = (
        (unit_norm * norm_gain + norm_shift)
        .astype(jnp.bfloat16)
        .reshape(rows_dev * col_count, channels)
    )
    normed_all = lax.all_gather(normed, "rows", axis=0, tiled=True)
    pre_act = jnp.dot(normed_all, up_weight, preferred_element_type=jnp.float32) + up_bias
    hidden = gelu_value(pre_act).astype(jnp.bfloat16)
    down_grad = contract(hidden, cot_all, 0, 0)
    hid_grad = contract(cot_all, down_weight, 1, 1)
    act_grad = (hid_grad * gelu_slope(pre_act)).astype(jnp.bfloat16)
    up_bias_grad = jnp.sum(act_grad.astype(jnp.float32), axis=0)
    up_grad = contract(normed_all, act_grad, 0, 0)
    norm_grad = lax.psum_scatter(
        contract(act_grad, up_weight, 1, 1), "rows", scatter_dimension=0, tiled=True
    ).reshape(rows_dev, col_count, channels)
    gain_part = jnp.sum(norm_grad * unit_norm, axis=(0, 1))
    shift_part = jnp.sum(norm_grad, axis=(0, 1))
    conv_grad = norm_back(norm_grad, unit_norm, inv_std, norm_gain)
    bias_part = jnp.sum(conv_grad, axis=(0, 1))
    kernel_rows = []
    for tap_row in range(7):
        kernel_cols = []
        for tap_col in range(7):
            kernel_cols.append(
                jnp.sum(
                    conv_grad
                    * padded[tap_row : tap_row + rows_dev, tap_col : tap_col + col_count, :],
                    axis=(0, 1),
                )
            )
        kernel_rows.append(jnp.stack(kernel_cols))
    kernel_part = jnp.stack(kernel_rows)
    near_grad = extended(conv_grad.astype(jnp.bfloat16), (("rows", 0),), 3).astype(conv_grad.dtype)
    grad_padded = pad_columns(near_grad * row_mask)
    back_term = depthwise_back(grad_padded, depth_kernel, rows_dev, col_count)
    input_grad = (cotangent.astype(jnp.float32) + back_term).astype(jnp.bfloat16)
    gain_grad, shift_grad, kernel_grad, depth_bias_grad = lax.psum(
        (gain_part, shift_part, kernel_part, bias_part), "rows"
    )
    return (
        input_grad,
        up_grad,
        up_bias_grad,
        down_grad,
        kernel_grad,
        depth_bias_grad,
        gain_grad,
        shift_grad,
    )


def solution(mesh):
    in_specs = (
        P(("groups", "rows"), None, None),
        P(("groups", "rows"), None, None),
        P(),
        P(),
        P(),
        P(),
        P(None, "rows"),
        P("rows"),
        P("rows", None),
        P(),
    )
    out_specs = (
        P(("groups", "rows"), None, None),
        P("groups", "rows"),
        P(("groups", "rows")),
        P(("groups", "rows"), None),
        P("groups", None, None),
        P("groups"),
        P("groups"),
        P("groups"),
    )
    return jax.shard_map(
        on_device, mesh=mesh, in_specs=in_specs, out_specs=out_specs, check_vma=False
    )
```

profile of v0, /device:TPU:0, one launch (start us, length us, event | category | flops | bytes accessed | tf_op | source)
XLA Modules:
  0.0 296.4 jit_solution(8445374431140622717)
XLA Ops:
  8.7 5.1 %collective-permute-start.1 = (bf16[3,4,3072]{2,1,0:T(4,128)(2,1)S(1)}, bf16[3,4,3072]{2,1,0:T(4,128)(2,1)S(1)}, u32[]{:S(2)}, u32[]{:S(2)}) collective-permute-start(bf16[3,4,3072]{2,1,0:T(4,128)(2,1)S(1)} %get-tuple-element.121), channel_id=1, source_target_pairs={{1,0},{2,1},{3,2},{4,3},{5,4},{6,5},{7,6},{8,7},{9,8},{10,9},{11,1... | collective-permute-start | bytes 221192 | tf_op jit(solution)/shard_map/ppermute | solution.py:18
  13.8 1.7 fusion.105
  15.6 2.3 fusion.103
  18.1 2.8 fusion.104
  21.6 1.1 convert_multiply_fusion.1
  22.7 5.2 %fusion.102 = (f32[4,4]{1,0:T(4,128)S(1)}, f32[4,4,3072]{2,1,0:T(4,128)S(1)}) fusion(f32[3072]{0:T(1024)S(1)} %copy-done.85, f32[3072]{0:T(1024)S(1)} %bitcast.139, f32[3072]{0:T(1024)S(1)} %bitcast.141, f32[3072]{0:T(1024)S(1)} %bitcast.145, f32[10,4,3072]{2,1,0:T(4,128)S(1)} %convert_multiply_fusion.1, f32[3072]{0:T(1024)S(1)} %bitcast.147, ...), kind=kLoop, calls=%fused_computation.279 | loop fusion | flops 4866032 | bytes 2678848 | tf_op jit(solution)/shard_map/reduce_sum | solution.py:72
  30.3 37.9 %all-gather.5.cloned.1.call-done = bf16[256,3072]{1,0:T(8,128)(2,1)} async-done(((bf16[16,3072]{1,0:T(8,128)(2,1)}), bf16[256,3072]{1,0:T(8,128)(2,1)}) %all-gather.5.cloned.1.call-update) | async-done | bytes 1572880 | tf_op jit(solution)/shard_map/all_gather | solution.py:127
  68.2 4.2 %convolution_add_fusion = f32[256,768]{1,0:T(8,128)S(1)} fusion(bf16[256,3072]{1,0:T(8,128)(2,1)} %all-gather.5.cloned.1.call-done, bf16[3072,768]{1,0:T(8,128)(2,1)} %param.16, f32[768]{0:T(1024)S(1)} %copy-done.88), kind=kOutput, calls=%fused_computation.85 | convolution fusion | flops 1208156160 | bytes 7080960 | tf_op jit(solution)/shard_map/dot_general | solution.py:128
  72.4 37.2 %all-gather.3.cloned.1.call-done = bf16[256,3072]{1,0:T(8,128)(2,1)} async-done(((bf16[16,3072]{1,0:T(8,128)(2,1)}), bf16[256,3072]{1,0:T(8,128)(2,1)}) %all-gather.3.cloned.1.call-update) | async-done | bytes 1572880 | tf_op jit(solution)/shard_map/all_gather | solution.py:117
  109.7 5.0 %convert_reduce_fusion = (f32[768]{0:T(1024)}, bf16[256,768]{1,0:T(8,128)(2,1)S(1)}) fusion(f32[256,768]{1,0:T(8,128)S(1)} %convolution_add_fusion, bf16[256,3072]{1,0:T(8,128)(2,1)} %all-gather.3.cloned.1.call-done, bf16[768,3072]{1,0:T(8,128)(2,1)} %param.18), kind=kOutput, calls=%fused_computation.93 | convolution fusion | flops 1210318080 | bytes 7474176 | tf_op jit(solution)/shard_map/dot_general | solution.py:35
  114.6 5.4 %fusion.108 = f32[256,3072]{1,0:T(8,128)} fusion(bf16[256,768]{1,0:T(8,128)(2,1)S(1)} %get-tuple-element.123, bf16[3072,768]{1,0:T(8,128)(2,1)} %param.16), kind=kOutput, calls=%fused_computation.285 | convolution fusion | flops 1207959552 | bytes 8257536 | tf_op jit(solution)/shard_map/dot_general | solution.py:35
  120.3 1.2 copy-done
  121.5 5.2 %fusion.109 = f32[3072,768]{1,0:T(8,128)} fusion(bf16[256,3072]{1,0:T(8,128)(2,1)S(1)} %copy-done, bf16[256,768]{1,0:T(8,128)(2,1)S(1)} %get-tuple-element.123), kind=kOutput, calls=%fused_computation.286 | convolution fusion | flops 1207959552 | bytes 11403264 | tf_op jit(solution)/shard_map/dot_general | solution.py:35
  126.7 5.2 %fusion.5 = f32[768,3072]{1,0:T(8,128)} fusion(bf16[256,3072]{1,0:T(8,128)(2,1)S(1)} %copy-done.1, f32[256,768]{1,0:T(8,128)S(1)} %convolution_add_fusion), kind=kOutput, calls=%fused_computation.97 | convolution fusion | flops 1208942592 | bytes 11796480 | tf_op jit(solution)/shard_map/dot_general | solution.py:35
  131.9 53.5 %reduce-scatter.2.cloned.1.call-done = f32[16,3072]{1,0:T(8,128)} async-done(((f32[256,3072]{1,0:T(8,128)}), f32[16,3072]{1,0:T(8,128)}) %reduce-scatter.2.cloned.1.call-update) | async-done | bytes 196624 | tf_op jit(solution)/shard_map/reduce_scatter | solution.py:135
  185.4 1.1 fusion.101
  187.8 1.5 multiply_reduce_fusion.1
  189.3 1.0 multiply_reduce_fusion.37
  190.3 1.3 multiply_reduce_fusion.19
  191.8 4.4 %collective-permute-start.3 = (bf16[3,4,3072]{2,1,0:T(4,128)(2,1)S(1)}, bf16[3,4,3072]{2,1,0:T(4,128)(2,1)S(1)}, u32[]{:S(2)}, u32[]{:S(2)}) collective-permute-start(bf16[3,4,3072]{2,1,0:T(4,128)(2,1)S(1)} %get-tuple-element.119), channel_id=1, source_target_pairs={{1,0},{2,1},{3,2},{4,3},{5,4},{6,5},{7,6},{8,7},{9,8},{10,9},{11,1... | collective-permute-start | bytes 221192 | tf_op jit(solution)/shard_map/ppermute | solution.py:18
  198.6 58.5 %all-reduce.2 = (f32[3072]{0:T(1024)}, f32[3072]{0:T(1024)}, f32[3072]{0:T(1024)}) all-reduce(f32[3072]{0:T(1024)S(1)} %get-tuple-element.61, f32[3072]{0:T(1024)S(1)} %get-tuple-element.57, f32[3072]{0:T(1024)S(1)} %get-tuple-element.59), channel_id=1, replica_groups=mesh['groups'=2,'rows'=16] {'rows'}, use_global_device_ids=true, to_apply=%region_57.58 | all-reduce | flops 9216 | bytes 73728 | tf_op jit(solution)/shard_map/psum | solution.py:159
  258.3 4.2 %fusion.8 = bf16[4,4,3072]{2,1,0:T(4,128)(2,1)} fusion(bf16[4,4,3072]{2,1,0:T(4,128)(2,1)S(1)} %copy-done.3, f32[10,4,3072]{2,1,0:T(4,128)S(1)} %convert_multiply_fusion, f32[3072]{0:T(1024)S(1)} %bitcast.140, f32[3072]{0:T(1024)S(1)} %bitcast.142, f32[3072]{0:T(1024)S(1)} %bitcast.146, f32[3072]{0:T(1024)S(1)} %bitcast.148, f32[3072]{0:T(1024)S(1)} %bitcast.150, ...), kind=kLoop, calls=%fused_computation.102 | loop fusion | flops 4915200 | bytes 2666496 | tf_op jit(solution)/shard_map/convert_element_type | solution.py:158
  262.6 25.3 %all-reduce.5.cloned.1.call-done = f32[7,7,3072]{2,1,0:T(8,128)} async-done(((f32[7,7,3072]{2,1,0:T(8,128)}), f32[7,7,3072]{2,1,0:T(8,128)}) %all-reduce.5.cloned.1.call-update) | async-done | bytes 602128 | tf_op jit(solution)/shard_map/psum | solution.py:159
  287.9 2.0 copy.25
  (221 shorter events, 8.8 us)
Async XLA Ops:
  7.2 61.0 %all-gather.5.cloned.1.call-start = ((), (), s32[]{:S(2)}) async-start(), calls=%async_computation.2 | async-start | bytes 1671168 | tf_op jit(solution)/shard_map/all_gather | solution.py:127
  8.2 13.4 %collective-permute-start = (bf16[3,4,3072]{2,1,0:T(4,128)(2,1)S(1)}, bf16[3,4,3072]{2,1,0:T(4,128)(2,1)S(1)}, u32[]{:S(2)}, u32[]{:S(2)}) collective-permute-start(bf16[3,4,3072]{2,1,0:T(4,128)(2,1)S(1)} %get-tuple-element.120), channel_id=1, source_target_pairs={{0,1},{1,2},{2,3},{3,4},{4,5},{5,6},{6,7},{7,8},{8,9},{9,10},{10,1... | collective-permute-start | bytes 221192 | tf_op jit(solution)/shard_map/ppermute | solution.py:16
  8.7 12.9 %collective-permute-start.1 = (bf16[3,4,3072]{2,1,0:T(4,128)(2,1)S(1)}, bf16[3,4,3072]{2,1,0:T(4,128)(2,1)S(1)}, u32[]{:S(2)}, u32[]{:S(2)}) collective-permute-start(bf16[3,4,3072]{2,1,0:T(4,128)(2,1)S(1)} %get-tuple-element.121), channel_id=1, source_target_pairs={{1,0},{2,1},{3,2},{4,3},{5,4},{6,5},{7,6},{8,7},{9,8},{10,9},{11,1... | collective-permute-start | bytes 221192 | tf_op jit(solution)/shard_map/ppermute | solution.py:18
  29.5 80.2 %all-gather.3.cloned.1.call-start = ((), (), s32[]{:S(2)}) async-start(), calls=%async_computation.1 | async-start | bytes 1671168 | tf_op jit(solution)/shard_map/all_gather | solution.py:117
  30.3 155.1 %reduce-scatter.2.cloned.1.call-start = ((), (), s32[]{:S(2)}) async-start(), calls=%async_computation.3 | async-start | bytes 3342336 | tf_op jit(solution)/shard_map/reduce_scatter | solution.py:135
  120.1 167.8 %all-reduce.5.cloned.1.call-start = ((), (), s32[]{:S(2)}) async-start(), calls=%async_computation.4 | async-start | bytes 1376256 | tf_op jit(solution)/shard_map/psum | solution.py:159
  191.7 65.4 %collective-permute-start.2 = (bf16[3,4,3072]{2,1,0:T(4,128)(2,1)S(1)}, bf16[3,4,3072]{2,1,0:T(4,128)(2,1)S(1)}, u32[]{:S(2)}, u32[]{:S(2)}) collective-permute-start(bf16[3,4,3072]{2,1,0:T(4,128)(2,1)S(1)} %get-tuple-element.118), channel_id=1, source_target_pairs={{0,1},{1,2},{2,3},{3,4},{4,5},{5,6},{6,7},{7,8},{8,9},{9,10},{10,1... | collective-permute-start | bytes 221192 | tf_op jit(solution)/shard_map/ppermute | solution.py:16
  191.8 65.3 %collective-permute-start.3 = (bf16[3,4,3072]{2,1,0:T(4,128)(2,1)S(1)}, bf16[3,4,3072]{2,1,0:T(4,128)(2,1)S(1)}, u32[]{:S(2)}, u32[]{:S(2)}) collective-permute-start(bf16[3,4,3072]{2,1,0:T(4,128)(2,1)S(1)} %get-tuple-element.119), channel_id=1, source_target_pairs={{1,0},{2,1},{3,2},{4,3},{5,4},{6,5},{7,6},{8,7},{9,8},{10,9},{11,1... | collective-permute-start | bytes 221192 | tf_op jit(solution)/shard_map/ppermute | solution.py:18
  196.4 61.6 %copy-start.6 = (f32[1,1,3072]{2,1,0:T(1,128)S(1)}, f32[1,1,3072]{2,1,0:T(1,128)}, u32[]{:S(2)}) copy-start(f32[1,1,3072]{2,1,0:T(1,128)} %copy-done.5) | copy-start | bytes 36868
  196.4 61.6 %copy-start.8 = (f32[1,1,3072]{2,1,0:T(1,128)S(1)}, f32[1,1,3072]{2,1,0:T(1,128)}, u32[]{:S(2)}) copy-start(f32[1,1,3072]{2,1,0:T(1,128)} %copy-done.7) | copy-start | bytes 36868
  196.4 61.6 %copy-start.10 = (f32[1,1,3072]{2,1,0:T(1,128)S(1)}, f32[1,1,3072]{2,1,0:T(1,128)}, u32[]{:S(2)}) copy-start(f32[1,1,3072]{2,1,0:T(1,128)} %copy-done.9) | copy-start | bytes 36868
  196.4 61.6 %copy-start.12 = (f32[1,1,3072]{2,1,0:T(1,128)S(1)}, f32[1,1,3072]{2,1,0:T(1,128)}, u32[]{:S(2)}) copy-start(f32[1,1,3072]{2,1,0:T(1,128)} %copy-done.11) | copy-start | bytes 36868
  196.4 61.6 %copy-start.14 = (f32[1,1,3072]{2,1,0:T(1,128)S(1)}, f32[1,1,3072]{2,1,0:T(1,128)}, u32[]{:S(2)}) copy-start(f32[1,1,3072]{2,1,0:T(1,128)} %copy-done.13) | copy-start | bytes 36868
  196.4 61.6 %copy-start.16 = (f32[1,1,3072]{2,1,0:T(1,128)S(1)}, f32[1,1,3072]{2,1,0:T(1,128)}, u32[]{:S(2)}) copy-start(f32[1,1,3072]{2,1,0:T(1,128)} %copy-done.15) | copy-start | bytes 36868
  196.4 61.6 %copy-start.18 = (f32[1,1,3072]{2,1,0:T(1,128)S(1)}, f32[1,1,3072]{2,1,0:T(1,128)}, u32[]{:S(2)}) copy-start(f32[1,1,3072]{2,1,0:T(1,128)} %copy-done.17) | copy-start | bytes 36868
  196.4 61.6 %copy-start.20 = (f32[1,1,3072]{2,1,0:T(1,128)S(1)}, f32[1,1,3072]{2,1,0:T(1,128)}, u32[]{:S(2)}) copy-start(f32[1,1,3072]{2,1,0:T(1,128)} %copy-done.19) | copy-start | bytes 36868
  196.4 61.6 %copy-start.22 = (f32[1,1,3072]{2,1,0:T(1,128)S(1)}, f32[1,1,3072]{2,1,0:T(1,128)}, u32[]{:S(2)}) copy-start(f32[1,1,3072]{2,1,0:T(1,128)} %copy-done.21) | copy-start | bytes 36868
  196.4 61.6 %copy-start.24 = (f32[1,1,3072]{2,1,0:T(1,128)S(1)}, f32[1,1,3072]{2,1,0:T(1,128)}, u32[]{:S(2)}) copy-start(f32[1,1,3072]{2,1,0:T(1,128)} %copy-done.23) | copy-start | bytes 36868
  196.5 61.6 %copy-start.26 = (f32[1,1,3072]{2,1,0:T(1,128)S(1)}, f32[1,1,3072]{2,1,0:T(1,128)}, u32[]{:S(2)}) copy-start(f32[1,1,3072]{2,1,0:T(1,128)} %copy-done.25) | copy-start | bytes 36868
  196.5 61.6 %copy-start.28 = (f32[1,1,3072]{2,1,0:T(1,128)S(1)}, f32[1,1,3072]{2,1,0:T(1,128)}, u32[]{:S(2)}) copy-start(f32[1,1,3072]{2,1,0:T(1,128)} %copy-done.27) | copy-start | bytes 36868
  196.5 61.6 %copy-start.30 = (f32[1,1,3072]{2,1,0:T(1,128)S(1)}, f32[1,1,3072]{2,1,0:T(1,128)}, u32[]{:S(2)}) copy-start(f32[1,1,3072]{2,1,0:T(1,128)} %copy-done.29) | copy-start | bytes 36868
  196.5 61.6 %copy-start.32 = (f32[1,1,3072]{2,1,0:T(1,128)S(1)}, f32[1,1,3072]{2,1,0:T(1,128)}, u32[]{:S(2)}) copy-start(f32[1,1,3072]{2,1,0:T(1,128)} %copy-done.31) | copy-start | bytes 36868
  196.5 61.6 %copy-start.34 = (f32[1,1,3072]{2,1,0:T(1,128)S(1)}, f32[1,1,3072]{2,1,0:T(1,128)}, u32[]{:S(2)}) copy-start(f32[1,1,3072]{2,1,0:T(1,128)} %copy-done.33) | copy-start | bytes 36868
  196.5 61.6 %copy-start.36 = (f32[1,1,3072]{2,1,0:T(1,128)S(1)}, f32[1,1,3072]{2,1,0:T(1,128)}, u32[]{:S(2)}) copy-start(f32[1,1,3072]{2,1,0:T(1,128)} %copy-done.35) | copy-start | bytes 36868
  (73 other events, 1978.4 us)
Sparse Core Ops, SparseCore 0:
  29.6 38.5 all-gather.4
  71.1 38.5 all-gather.2
  120.2 65.0 reduce-scatter.1
  198.7 89.1 all-reduce.4
where the time goes:
time: 297 us; the launch traced here: 296 us
  waiting for transfers between devices  154 us (52%)
  blocking collectives  58.5 us (20%)
  matrix products  25 us (8%)
  other arithmetic  17.7 us (6%)
  local copies, waits for them, and re-layouts  15.6 us (5%)
  between operations  15.3 us (5%)
  starting transfers between devices  10.4 us (4%)
    psum x1, blocking collectives, on_device(): lax.psum((gain_part, shift_part, kernel_part, bias_part), 'rows')  58.5 us
    reduce_scatter x1, waiting for transfers between devices, on_device(): lax.psum_scatter(contract(act_grad, up_weight, 1, 1), 'rows', scatter_dim...  53.5 us
    all_gather x1, waiting for transfers between devices, on_device(): normed_all = lax.all_gather(normed, 'rows', axis=0, tiled=True)  37.9 us
    all_gather x1, waiting for transfers between devices, on_device(): cot_all = lax.all_gather(cot_scaled, 'rows', axis=0, tiled=True)  37.2 us
    psum x1, waiting for transfers between devices, on_device(): lax.psum((gain_part, shift_part, kernel_part, bias_part), 'rows')  25.3 us
    dot_general x4, matrix products, contract(): lax.dot_general(left, right, (((left_dim,), (right_dim,)), ((), ())), pre...  20.8 us
    ppermute x2, starting transfers between devices, extended(): lax.ppermute(head, axis, [((i + 1) % count, i) for i in range(count)])  9.49 us
  transfers between devices with their start and end apart: 8, of which 4 were waited for; matrix products, arithmetic and copies ran while one was open for 10% of the time, Pallas kernels for 0%

commit v1 on v0

--- a/solution.py
+++ b/solution.py
@@ -114,7 +114,23 @@
         .astype(jnp.bfloat16)
         .reshape(rows_dev * col_count, channels)
     )
-    cot_all = lax.all_gather(cot_scaled, "rows", axis=0, tiled=True)
+    ways, here, lap = (lax.axis_size("rows"), lax.axis_index("rows"), cot_scaled.shape[0])
+    dims = [n * ways if d == 0 else n for d, n in enumerate(cot_scaled.shape)]
+    full = lax.dynamic_update_slice_in_dim(
+        jnp.zeros(dims, cot_scaled.dtype), cot_scaled, here * lap, axis=0
+    )
+    going_up = going_down = cot_scaled
+    for far in range(1, ways // 2 + 1):
+        going_up = lax.ppermute(going_up, "rows", [(d, (d + 1) % ways) for d in range(ways)])
+        full = lax.dynamic_update_slice_in_dim(full, going_up, (here - far) % ways * lap, axis=0)
+        if 2 * far < ways:
+            going_down = lax.ppermute(
+                going_down, "rows", [(d, (d - 1) % ways) for d in range(ways)]
+            )
+            full = lax.dynamic_update_slice_in_dim(
+                full, going_down, (here + far) % ways * lap, axis=0
+            )
+    cot_all = full
     near_rows = extended(features, (("rows", 0),), 3)
     padded = pad_columns(near_rows.astype(jnp.float32) * row_mask)
     conv_out = depthwise(padded, depth_kernel, depth_bias, rows_dev, col_count)

time: 297 us -> 272 us (0.916)
  waiting for transfers between devices: 154 us -> 105 us
  starting transfers between devices: 10.4 us -> 40.6 us
  local copies, waits for them, and re-layouts: 15.6 us -> 10 us
    all_gather x1, waiting for transfers between devices: 37.9 us -> 0.02 us  [on_device(): normed_all = lax.all_gather(normed, 'rows', axis=0, tiled=True)]
    all_gather x1 -> x0, waiting for transfers between devices: 37.2 us -> none  [on_device(): cot_all = lax.all_gather(cot_scaled, 'rows', axis=0, tiled=True)]
    ppermute x0 -> x15, starting transfers between devices: none -> 31.2 us  [the longest x7 31.2 us: on_device(): lax.ppermute(going_down, 'rows', [(d, (d - 1) % ways) for d in range(ways)])]
    ppermute x0 -> x15, waiting for transfers between devices: none -> 26.7 us  [the longest x8 17.9 us: on_device(): lax.ppermute(going_up, 'rows', [(d, (d + 1) % ways) for d in range(ways)])]
  transfers between devices with their start and end apart: 8 -> 22, of which waited for: 4 -> 13; matrix products, arithmetic and copies ran while one was open for 10% -> 11% of each run, Pallas kernels for 0% -> 0%
where the time goes in v1:
time: 272 us; the launch traced here: 271 us
  waiting for transfers between devices  105 us (39%)
  blocking collectives  58.5 us (22%)
  starting transfers between devices  40.6 us (15%)
  matrix products  23.8 us (9%)
  other arithmetic  17.9 us (7%)
  between operations  15.5 us (6%)
  local copies, waits for them, and re-layouts  10 us (4%)
    psum x1, blocking collectives, on_device(): lax.psum((gain_part, shift_part, kernel_part, bias_part), 'rows')  58.5 us
    reduce_scatter x1, waiting for transfers between devices, on_device(): lax.psum_scatter(contract(act_grad, up_weight, 1, 1), 'rows', scatter_dim...  52.4 us
    ppermute x7, starting transfers between devices, on_device(): lax.ppermute(going_down, 'rows', [(d, (d - 1) % ways) for d in range(ways)])  31.2 us
    psum x1, waiting for transfers between devices, on_device(): lax.psum((gain_part, shift_part, kernel_part, bias_part), 'rows')  25.6 us
    dot_general x4, matrix products, contract(): lax.dot_general(left, right, (((left_dim,), (right_dim,)), ((), ())), pre...  19.4 us
    ppermute x8, waiting for transfers between devices, on_device(): lax.ppermute(going_up, 'rows', [(d, (d + 1) % ways) for d in range(ways)])  17.9 us
    ppermute x2, starting transfers between devices, extended(): lax.ppermute(head, axis, [((i + 1) % count, i) for i in range(count)])  8.92 us
    ppermute x7, waiting for transfers between devices, on_device(): lax.ppermute(going_down, 'rows', [(d, (d - 1) % ways) for d in range(ways)])  8.75 us
  transfers between devices with their start and end apart: 22, of which 13 were waited for; matrix products, arithmetic and copies ran while one was open for 11% of the time, Pallas kernels for 0%

profile of v1, /device:TPU:0, one launch (start us, length us, event | category | flops | bytes accessed | tf_op | source)
XLA Modules:
  0.0 271.1 jit_solution(14453638341192140194)
XLA Ops:
  8.3 5.5 %collective-permute-start.3 = (bf16[16,3072]{1,0:T(8,128)(2,1)S(1)}, bf16[16,3072]{1,0:T(8,128)(2,1)S(1)}, u32[]{:S(2)}, u32[]{:S(2)}) collective-permute-start(bf16[16,3072]{1,0:T(8,128)(2,1)S(1)} %reshape.89), channel_id=1, source_target_pairs={{0,15},{1,0},{2,1},{3,2},{4,3},{5,4},{6,5},{7,6},{8,7},{9,8},{10,9... | collective-permute-start | bytes 294920 | tf_op jit(solution)/shard_map/ppermute | solution.py:127
  14.8 4.5 %collective-permute-start.1 = (bf16[3,4,3072]{2,1,0:T(4,128)(2,1)S(1)}, bf16[3,4,3072]{2,1,0:T(4,128)(2,1)S(1)}, u32[]{:S(2)}, u32[]{:S(2)}) collective-permute-start(bf16[3,4,3072]{2,1,0:T(4,128)(2,1)S(1)} %get-tuple-element.121), channel_id=1, source_target_pairs={{1,0},{2,1},{3,2},{4,3},{5,4},{6,5},{7,6},{8,7},{9,8},{10,9},{11,1... | collective-permute-start | bytes 221192 | tf_op jit(solution)/shard_map/ppermute | solution.py:18
  24.2 5.1 %fusion.102 = (f32[4,4]{1,0:T(4,128)S(1)}, f32[4,4,3072]{2,1,0:T(4,128)S(1)}) fusion(f32[3072]{0:T(1024)S(1)} %copy-done.85, f32[3072]{0:T(1024)S(1)} %bitcast.141, f32[3072]{0:T(1024)S(1)} %bitcast.143, f32[3072]{0:T(1024)S(1)} %bitcast.147, f32[10,4,3072]{2,1,0:T(4,128)S(1)} %convert_multiply_fusion.1, f32[3072]{0:T(1024)S(1)} %bitcast.149, ...), kind=kLoop, calls=%fused_computation.295 | loop fusion | flops 4866032 | bytes 2678848 | tf_op jit(solution)/shard_map/reduce_sum | solution.py:72
  30.7 2.7 collective-permute-start.5
  33.4 2.2 collective-permute-done.5
  35.5 4.6 %collective-permute-start.7 = (bf16[16,3072]{1,0:T(8,128)(2,1)S(1)}, bf16[16,3072]{1,0:T(8,128)(2,1)S(1)}, u32[]{:S(2)}, u32[]{:S(2)}) collective-permute-start(bf16[16,3072]{1,0:T(8,128)(2,1)S(1)} %collective-permute-done.5), channel_id=1, source_target_pairs={{0,15},{1,0},{2,1},{3,2},{4,3},{5,4},{6,5},{7,6},{8,7},{9,8},{10,9... | collective-permute-start | bytes 294920 | tf_op jit(solution)/shard_map/ppermute | solution.py:127
  40.2 2.2 collective-permute-done.7
  42.4 4.6 %collective-permute-start.9 = (bf16[16,3072]{1,0:T(8,128)(2,1)S(1)}, bf16[16,3072]{1,0:T(8,128)(2,1)S(1)}, u32[]{:S(2)}, u32[]{:S(2)}) collective-permute-start(bf16[16,3072]{1,0:T(8,128)(2,1)S(1)} %collective-permute-done.7), channel_id=1, source_target_pairs={{0,15},{1,0},{2,1},{3,2},{4,3},{5,4},{6,5},{7,6},{8,7},{9,8},{10,9... | collective-permute-start | bytes 294920 | tf_op jit(solution)/shard_map/ppermute | solution.py:127
  49.4 4.6 %collective-permute-start.11 = (bf16[16,3072]{1,0:T(8,128)(2,1)S(1)}, bf16[16,3072]{1,0:T(8,128)(2,1)S(1)}, u32[]{:S(2)}, u32[]{:S(2)}) collective-permute-start(bf16[16,3072]{1,0:T(8,128)(2,1)S(1)} %collective-permute-done.9), channel_id=1, source_target_pairs={{0,15},{1,0},{2,1},{3,2},{4,3},{5,4},{6,5},{7,6},{8,7},{9,8},{10,9... | collective-permute-start | bytes 294920 | tf_op jit(solution)/shard_map/ppermute | solution.py:127
  56.2 4.6 %collective-permute-start.13 = (bf16[16,3072]{1,0:T(8,128)(2,1)S(1)}, bf16[16,3072]{1,0:T(8,128)(2,1)S(1)}, u32[]{:S(2)}, u32[]{:S(2)}) collective-permute-start(bf16[16,3072]{1,0:T(8,128)(2,1)S(1)} %collective-permute-done.11), channel_id=1, source_target_pairs={{0,15},{1,0},{2,1},{3,2},{4,3},{5,4},{6,5},{7,6},{8,7},{9,8},{10,9... | collective-permute-start | bytes 294920 | tf_op jit(solution)/shard_map/ppermute | solution.py:127
  63.0 4.6 %collective-permute-start.15 = (bf16[16,3072]{1,0:T(8,128)(2,1)S(1)}, bf16[16,3072]{1,0:T(8,128)(2,1)S(1)}, u32[]{:S(2)}, u32[]{:S(2)}) collective-permute-start(bf16[16,3072]{1,0:T(8,128)(2,1)S(1)} %collective-permute-done.13), channel_id=1, source_target_pairs={{0,15},{1,0},{2,1},{3,2},{4,3},{5,4},{6,5},{7,6},{8,7},{9,8},{10,9... | collective-permute-start | bytes 294920 | tf_op jit(solution)/shard_map/ppermute | solution.py:127
  67.6 2.3 collective-permute-done.12
  69.9 6.7 %collective-permute-done.14 = bf16[16,3072]{1,0:T(8,128)(2,1)S(1)} collective-permute-done((bf16[16,3072]{1,0:T(8,128)(2,1)S(1)}, bf16[16,3072]{1,0:T(8,128)(2,1)S(1)}, u32[]{:S(2)}, u32[]{:S(2)}) %collective-permute-start.14) | collective-permute-done | bytes 98336 | tf_op jit(solution)/shard_map/ppermute | solution.py:124
  76.7 6.7 %collective-permute-done.16 = bf16[16,3072]{1,0:T(8,128)(2,1)S(1)} collective-permute-done((bf16[16,3072]{1,0:T(8,128)(2,1)S(1)}, bf16[16,3072]{1,0:T(8,128)(2,1)S(1)}, u32[]{:S(2)}, u32[]{:S(2)}) %collective-permute-start.16) | collective-permute-done | bytes 98336 | tf_op jit(solution)/shard_map/ppermute | solution.py:124
  83.4 4.3 %convolution_add_fusion = f32[256,768]{1,0:T(8,128)S(1)} fusion(bf16[256,3072]{1,0:T(8,128)(2,1)} %all-gather.2.cloned.1.call-done, bf16[3072,768]{1,0:T(8,128)(2,1)} %param.16, f32[768]{0:T(1024)S(1)} %copy-done.87), kind=kOutput, calls=%fused_computation.85 | convolution fusion | flops 1208156160 | bytes 7080960 | tf_op jit(solution)/shard_map/dot_general | solution.py:144
  87.8 4.6 %convert_reduce_fusion = (f32[768]{0:T(1024)}, bf16[256,768]{1,0:T(8,128)(2,1)S(1)}) fusion(f32[256,768]{1,0:T(8,128)S(1)} %convolution_add_fusion, bf16[256,3072]{1,0:T(8,128)(2,1)S(1)} %constant_dynamic-update-slice_fusion, bf16[768,3072]{1,0:T(8,128)(2,1)} %param.18), kind=kOutput, calls=%fused_computation.93 | convolution fusion | flops 1210318080 | bytes 7474176 | tf_op jit(solution)/shard_map/dot_general | solution.py:35
  92.4 3.1 %fusion.108 = f32[256,3072]{1,0:T(8,128)} fusion(bf16[256,768]{1,0:T(8,128)(2,1)S(1)} %get-tuple-element.123, bf16[3072,768]{1,0:T(8,128)(2,1)S(1)} %bitcast.122), kind=kOutput, calls=%fused_computation.301 | convolution fusion | flops 1207959552 | bytes 8257536 | tf_op jit(solution)/shard_map/dot_general | solution.py:35
  95.7 6.6 %fusion.109 = f32[3072,768]{1,0:T(8,128)} fusion(bf16[256,3072]{1,0:T(8,128)(2,1)} %all-gather.2.cloned.1.call-done, bf16[256,768]{1,0:T(8,128)(2,1)S(1)} %get-tuple-element.123), kind=kOutput, calls=%fused_computation.302 | convolution fusion | flops 1207959552 | bytes 11403264 | tf_op jit(solution)/shard_map/dot_general | solution.py:35
  102.3 5.2 %fusion.5 = f32[768,3072]{1,0:T(8,128)} fusion(bf16[256,3072]{1,0:T(8,128)(2,1)S(1)} %constant_dynamic-update-slice_fusion, f32[256,768]{1,0:T(8,128)S(1)} %convolution_add_fusion), kind=kOutput, calls=%fused_computation.97 | convolution fusion | flops 1208942592 | bytes 11796480 | tf_op jit(solution)/shard_map/dot_general | solution.py:35
  107.5 52.4 %reduce-scatter.2.cloned.1.call-done = f32[16,3072]{1,0:T(8,128)} async-done(((f32[256,3072]{1,0:T(8,128)}), f32[16,3072]{1,0:T(8,128)}) %reduce-scatter.2.cloned.1.call-update) | async-done | bytes 196624 | tf_op jit(solution)/shard_map/reduce_scatter | solution.py:151
  166.3 4.4 %collective-permute-start.18 = (bf16[3,4,3072]{2,1,0:T(4,128)(2,1)S(1)}, bf16[3,4,3072]{2,1,0:T(4,128)(2,1)S(1)}, u32[]{:S(2)}, u32[]{:S(2)}) collective-permute-start(bf16[3,4,3072]{2,1,0:T(4,128)(2,1)S(1)} %get-tuple-element.119), channel_id=1, source_target_pairs={{1,0},{2,1},{3,2},{4,3},{5,4},{6,5},{7,6},{8,7},{9,8},{10,9},{11,1... | collective-permute-start | bytes 221192 | tf_op jit(solution)/shard_map/ppermute | solution.py:18
  173.1 58.5 %all-reduce.2 = (f32[3072]{0:T(1024)}, f32[3072]{0:T(1024)}, f32[3072]{0:T(1024)}) all-reduce(f32[3072]{0:T(1024)S(1)} %get-tuple-element.61, f32[3072]{0:T(1024)S(1)} %get-tuple-element.57, f32[3072]{0:T(1024)S(1)} %get-tuple-element.59), channel_id=1, replica_groups=mesh['groups'=2,'rows'=16] {'rows'}, use_global_device_ids=true, to_apply=%region_57.58 | all-reduce | flops 9216 | bytes 73728 | tf_op jit(solution)/shard_map/psum | solution.py:175
  232.9 4.1 %fusion.8 = bf16[4,4,3072]{2,1,0:T(4,128)(2,1)} fusion(bf16[4,4,3072]{2,1,0:T(4,128)(2,1)S(1)} %copy-done.3, f32[10,4,3072]{2,1,0:T(4,128)S(1)} %convert_multiply_fusion, f32[3072]{0:T(1024)S(1)} %bitcast.142, f32[3072]{0:T(1024)S(1)} %bitcast.144, f32[3072]{0:T(1024)S(1)} %bitcast.148, f32[3072]{0:T(1024)S(1)} %bitcast.150, f32[3072]{0:T(1024)S(1)} %bitcast.152, ...), kind=kLoop, calls=%fused_computation.102 | loop fusion | flops 4915200 | bytes 2666496 | tf_op jit(solution)/shard_map/convert_element_type | solution.py:174
  237.0 25.6 %all-reduce.5.cloned.1.call-done = f32[7,7,3072]{2,1,0:T(8,128)} async-done(((f32[7,7,3072]{2,1,0:T(8,128)}), f32[7,7,3072]{2,1,0:T(8,128)}) %all-reduce.5.cloned.1.call-update) | async-done | bytes 602128 | tf_op jit(solution)/shard_map/psum | solution.py:175
  (268 shorter events, 25.9 us)
Async XLA Ops:
  7.2 76.2 %all-gather.2.cloned.1.call-start = ((), (), s32[]{:S(2)}) async-start(), calls=%async_computation.1 | async-start | bytes 1671168 | tf_op jit(solution)/shard_map/all_gather | solution.py:143
  8.3 22.4 %collective-permute-start.3 = (bf16[16,3072]{1,0:T(8,128)(2,1)S(1)}, bf16[16,3072]{1,0:T(8,128)(2,1)S(1)}, u32[]{:S(2)}, u32[]{:S(2)}) collective-permute-start(bf16[16,3072]{1,0:T(8,128)(2,1)S(1)} %reshape.89), channel_id=1, source_target_pairs={{0,15},{1,0},{2,1},{3,2},{4,3},{5,4},{6,5},{7,6},{8,7},{9,8},{10,9... | collective-permute-start | bytes 294920 | tf_op jit(solution)/shard_map/ppermute | solution.py:127
  13.8 19.6 %collective-permute-start.2 = (bf16[16,3072]{1,0:T(8,128)(2,1)S(1)}, bf16[16,3072]{1,0:T(8,128)(2,1)S(1)}, u32[]{:S(2)}, u32[]{:S(2)}) collective-permute-start(bf16[16,3072]{1,0:T(8,128)(2,1)S(1)} %reshape.89), channel_id=1, source_target_pairs={{0,1},{1,2},{2,3},{3,4},{4,5},{5,6},{6,7},{7,8},{8,9},{9,10},{10,1... | collective-permute-start | bytes 294920 | tf_op jit(solution)/shard_map/ppermute | solution.py:124
  14.8 8.4 %collective-permute-start = (bf16[3,4,3072]{2,1,0:T(4,128)(2,1)S(1)}, bf16[3,4,3072]{2,1,0:T(4,128)(2,1)S(1)}, u32[]{:S(2)}, u32[]{:S(2)}) collective-permute-start(bf16[3,4,3072]{2,1,0:T(4,128)(2,1)S(1)} %get-tuple-element.120), channel_id=1, source_target_pairs={{0,1},{1,2},{2,3},{3,4},{4,5},{5,6},{6,7},{7,8},{8,9},{9,10},{10,1... | collective-permute-start | bytes 221192 | tf_op jit(solution)/shard_map/ppermute | solution.py:16
  14.8 8.3 %collective-permute-start.1 = (bf16[3,4,3072]{2,1,0:T(4,128)(2,1)S(1)}, bf16[3,4,3072]{2,1,0:T(4,128)(2,1)S(1)}, u32[]{:S(2)}, u32[]{:S(2)}) collective-permute-start(bf16[3,4,3072]{2,1,0:T(4,128)(2,1)S(1)} %get-tuple-element.121), channel_id=1, source_target_pairs={{1,0},{2,1},{3,2},{4,3},{5,4},{6,5},{7,6},{8,7},{9,8},{10,9},{11,1... | collective-permute-start | bytes 221192 | tf_op jit(solution)/shard_map/ppermute | solution.py:18
  30.6 129.3 %reduce-scatter.2.cloned.1.call-start = ((), (), s32[]{:S(2)}) async-start(), calls=%async_computation.2 | async-start | bytes 3342336 | tf_op jit(solution)/shard_map/reduce_scatter | solution.py:151
  30.7 4.9 %collective-permute-start.5 = (bf16[16,3072]{1,0:T(8,128)(2,1)S(1)}, bf16[16,3072]{1,0:T(8,128)(2,1)S(1)}, u32[]{:S(2)}, u32[]{:S(2)}) collective-permute-start(bf16[16,3072]{1,0:T(8,128)(2,1)S(1)} %collective-permute-done.3), channel_id=1, source_target_pairs={{0,15},{1,0},{2,1},{3,2},{4,3},{5,4},{6,5},{7,6},{8,7},{9,8},{10,9... | collective-permute-start | bytes 294920 | tf_op jit(solution)/shard_map/ppermute | solution.py:127
  33.3 6.8 %collective-permute-start.4 = (bf16[16,3072]{1,0:T(8,128)(2,1)S(1)}, bf16[16,3072]{1,0:T(8,128)(2,1)S(1)}, u32[]{:S(2)}, u32[]{:S(2)}) collective-permute-start(bf16[16,3072]{1,0:T(8,128)(2,1)S(1)} %collective-permute-done.2), channel_id=1, source_target_pairs={{0,1},{1,2},{2,3},{3,4},{4,5},{5,6},{6,7},{7,8},{8,9},{9,10},{10,1... | collective-permute-start | bytes 294920 | tf_op jit(solution)/shard_map/ppermute | solution.py:124
  35.5 6.8 %collective-permute-start.7 = (bf16[16,3072]{1,0:T(8,128)(2,1)S(1)}, bf16[16,3072]{1,0:T(8,128)(2,1)S(1)}, u32[]{:S(2)}, u32[]{:S(2)}) collective-permute-start(bf16[16,3072]{1,0:T(8,128)(2,1)S(1)} %collective-permute-done.5), channel_id=1, source_target_pairs={{0,15},{1,0},{2,1},{3,2},{4,3},{5,4},{6,5},{7,6},{8,7},{9,8},{10,9... | collective-permute-start | bytes 294920 | tf_op jit(solution)/shard_map/ppermute | solution.py:127
  40.2 7.6 %collective-permute-start.6 = (bf16[16,3072]{1,0:T(8,128)(2,1)S(1)}, bf16[16,3072]{1,0:T(8,128)(2,1)S(1)}, u32[]{:S(2)}, u32[]{:S(2)}) collective-permute-start(bf16[16,3072]{1,0:T(8,128)(2,1)S(1)} %collective-permute-done.4), channel_id=1, source_target_pairs={{0,1},{1,2},{2,3},{3,4},{4,5},{5,6},{6,7},{7,8},{8,9},{9,10},{10,1... | collective-permute-start | bytes 294920 | tf_op jit(solution)/shard_map/ppermute | solution.py:124
  42.4 7.0 %collective-permute-start.9 = (bf16[16,3072]{1,0:T(8,128)(2,1)S(1)}, bf16[16,3072]{1,0:T(8,128)(2,1)S(1)}, u32[]{:S(2)}, u32[]{:S(2)}) collective-permute-start(bf16[16,3072]{1,0:T(8,128)(2,1)S(1)} %collective-permute-done.7), channel_id=1, source_target_pairs={{0,15},{1,0},{2,1},{3,2},{4,3},{5,4},{6,5},{7,6},{8,7},{9,8},{10,9... | collective-permute-start | bytes 294920 | tf_op jit(solution)/shard_map/ppermute | solution.py:127
  47.7 6.8 %collective-permute-start.8 = (bf16[16,3072]{1,0:T(8,128)(2,1)S(1)}, bf16[16,3072]{1,0:T(8,128)(2,1)S(1)}, u32[]{:S(2)}, u32[]{:S(2)}) collective-permute-start(bf16[16,3072]{1,0:T(8,128)(2,1)S(1)} %collective-permute-done.6), channel_id=1, source_target_pairs={{0,1},{1,2},{2,3},{3,4},{4,5},{5,6},{6,7},{7,8},{8,9},{9,10},{10,1... | collective-permute-start | bytes 294920 | tf_op jit(solution)/shard_map/ppermute | solution.py:124
  49.4 6.8 %collective-permute-start.11 = (bf16[16,3072]{1,0:T(8,128)(2,1)S(1)}, bf16[16,3072]{1,0:T(8,128)(2,1)S(1)}, u32[]{:S(2)}, u32[]{:S(2)}) collective-permute-start(bf16[16,3072]{1,0:T(8,128)(2,1)S(1)} %collective-permute-done.9), channel_id=1, source_target_pairs={{0,15},{1,0},{2,1},{3,2},{4,3},{5,4},{6,5},{7,6},{8,7},{9,8},{10,9... | collective-permute-start | bytes 294920 | tf_op jit(solution)/shard_map/ppermute | solution.py:127
  54.5 7.4 %collective-permute-start.10 = (bf16[16,3072]{1,0:T(8,128)(2,1)S(1)}, bf16[16,3072]{1,0:T(8,128)(2,1)S(1)}, u32[]{:S(2)}, u32[]{:S(2)}) collective-permute-start(bf16[16,3072]{1,0:T(8,128)(2,1)S(1)} %collective-permute-done.8), channel_id=1, source_target_pairs={{0,1},{1,2},{2,3},{3,4},{4,5},{5,6},{6,7},{7,8},{8,9},{9,10},{10,1... | collective-permute-start | bytes 294920 | tf_op jit(solution)/shard_map/ppermute | solution.py:124
  56.2 6.8 %collective-permute-start.13 = (bf16[16,3072]{1,0:T(8,128)(2,1)S(1)}, bf16[16,3072]{1,0:T(8,128)(2,1)S(1)}, u32[]{:S(2)}, u32[]{:S(2)}) collective-permute-start(bf16[16,3072]{1,0:T(8,128)(2,1)S(1)} %collective-permute-done.11), channel_id=1, source_target_pairs={{0,15},{1,0},{2,1},{3,2},{4,3},{5,4},{6,5},{7,6},{8,7},{9,8},{10,9... | collective-permute-start | bytes 294920 | tf_op jit(solution)/shard_map/ppermute | solution.py:127
  61.9 8.0 %collective-permute-start.12 = (bf16[16,3072]{1,0:T(8,128)(2,1)S(1)}, bf16[16,3072]{1,0:T(8,128)(2,1)S(1)}, u32[]{:S(2)}, u32[]{:S(2)}) collective-permute-start(bf16[16,3072]{1,0:T(8,128)(2,1)S(1)} %collective-permute-done.10), channel_id=1, source_target_pairs={{0,1},{1,2},{2,3},{3,4},{4,5},{5,6},{6,7},{7,8},{8,9},{9,10},{10,1... | collective-permute-start | bytes 294920 | tf_op jit(solution)/shard_map/ppermute | solution.py:124
  63.0 13.6 %collective-permute-start.15 = (bf16[16,3072]{1,0:T(8,128)(2,1)S(1)}, bf16[16,3072]{1,0:T(8,128)(2,1)S(1)}, u32[]{:S(2)}, u32[]{:S(2)}) collective-permute-start(bf16[16,3072]{1,0:T(8,128)(2,1)S(1)} %collective-permute-done.13), channel_id=1, source_target_pairs={{0,15},{1,0},{2,1},{3,2},{4,3},{5,4},{6,5},{7,6},{8,7},{9,8},{10,9... | collective-permute-start | bytes 294920 | tf_op jit(solution)/shard_map/ppermute | solution.py:127
  69.9 6.7 %collective-permute-start.14 = (bf16[16,3072]{1,0:T(8,128)(2,1)S(1)}, bf16[16,3072]{1,0:T(8,128)(2,1)S(1)}, u32[]{:S(2)}, u32[]{:S(2)}) collective-permute-start(bf16[16,3072]{1,0:T(8,128)(2,1)S(1)} %collective-permute-done.12), channel_id=1, source_target_pairs={{0,1},{1,2},{2,3},{3,4},{4,5},{5,6},{6,7},{7,8},{8,9},{9,10},{10,1... | collective-permute-start | bytes 294920 | tf_op jit(solution)/shard_map/ppermute | solution.py:124
  76.6 6.7 %collective-permute-start.16 = (bf16[16,3072]{1,0:T(8,128)(2,1)S(1)}, bf16[16,3072]{1,0:T(8,128)(2,1)S(1)}, u32[]{:S(2)}, u32[]{:S(2)}) collective-permute-start(bf16[16,3072]{1,0:T(8,128)(2,1)S(1)} %collective-permute-done.14), channel_id=1, source_target_pairs={{0,1},{1,2},{2,3},{3,4},{4,5},{5,6},{6,7},{7,8},{8,9},{9,10},{10,1... | collective-permute-start | bytes 294920 | tf_op jit(solution)/shard_map/ppermute | solution.py:124
  95.5 167.1 %all-reduce.5.cloned.1.call-start = ((), (), s32[]{:S(2)}) async-start(), calls=%async_computation.3 | async-start | bytes 1376256 | tf_op jit(solution)/shard_map/psum | solution.py:175
  166.3 65.4 %collective-permute-start.17 = (bf16[3,4,3072]{2,1,0:T(4,128)(2,1)S(1)}, bf16[3,4,3072]{2,1,0:T(4,128)(2,1)S(1)}, u32[]{:S(2)}, u32[]{:S(2)}) collective-permute-start(bf16[3,4,3072]{2,1,0:T(4,128)(2,1)S(1)} %get-tuple-element.118), channel_id=1, source_target_pairs={{0,1},{1,2},{2,3},{3,4},{4,5},{5,6},{6,7},{7,8},{8,9},{9,10},{10,1... | collective-permute-start | bytes 221192 | tf_op jit(solution)/shard_map/ppermute | solution.py:16
  166.3 65.3 %collective-permute-start.18 = (bf16[3,4,3072]{2,1,0:T(4,128)(2,1)S(1)}, bf16[3,4,3072]{2,1,0:T(4,128)(2,1)S(1)}, u32[]{:S(2)}, u32[]{:S(2)}) collective-permute-start(bf16[3,4,3072]{2,1,0:T(4,128)(2,1)S(1)} %get-tuple-element.119), channel_id=1, source_target_pairs={{1,0},{2,1},{3,2},{4,3},{5,4},{6,5},{7,6},{8,7},{9,8},{10,9},{11,1... | collective-permute-start | bytes 221192 | tf_op jit(solution)/shard_map/ppermute | solution.py:18
  171.2 61.2 %copy-start.3 = (bf16[4,4,3072]{2,1,0:T(4,128)(2,1)S(1)}, bf16[4,4,3072]{2,1,0:T(4,128)(2,1)}, u32[]{:S(2)}) copy-start(bf16[4,4,3072]{2,1,0:T(4,128)(2,1)} %param.11) | copy-start | bytes 294916
  171.2 61.2 %copy-start.6 = (f32[1,1,3072]{2,1,0:T(1,128)S(1)}, f32[1,1,3072]{2,1,0:T(1,128)}, u32[]{:S(2)}) copy-start(f32[1,1,3072]{2,1,0:T(1,128)} %copy-done.5) | copy-start | bytes 36868
  (88 other events, 2708.1 us)
Sparse Core Ops, SparseCore 0:
  30.7 41.1 all-gather.1
  95.6 64.2 reduce-scatter.1
  173.3 89.2 all-reduce.4
